TPU v7x, 768 devices: a whole 4x8x12 slice. The times are simulated.
768 devices in a mesh: ship: 64 (over x, y, core), truck: 12 (over z).
Axes of the slice: x: 4, y: 8, z: 12, core: 2. Of those that a mesh axis runs over, the one named last changes fastest.
Arguments:
- tile_cost: bfloat16 [512, 12, 256, 256], P('ship', 'truck')
- warm_plan: bfloat16 [512, 12, 256, 256], P('ship', 'truck'), may hold values from 0 to 1, as said below
- slot_ship: int32 [512, 12], P('ship', 'truck'), may hold values from -1 to 23, as said below
- slot_truck: int32 [512, 12], P('ship', 'truck'), may hold values from 0 to 5
- ship_load: float32 [2, 393216], P(None, 'ship'), may hold values from 0.5 to 2
- truck_limit: float32 [2, 18432], P(None, 'truck'), may hold values from 4096 to 16384
- warm_ship_price: float32 [393216], P('ship'), may hold values from 0 to 1
- warm_truck_price: float32 [2, 18432], P(None, 'truck'), may hold values from 0 to 1
Outputs:
- final_plan: float32 [512, 12, 256, 256], P('ship', 'truck')
- ship_price: float32 [393216], P('ship')
- truck_price: float32 [2, 18432], P(None, 'truck')
- primal_weight: float32 [], replicated
Inputs may be any that keep to these rules, and one draw needn't show every extreme that they name: `slot_ship`: on each device the live slots come first and name distinct blocks; at least 4 slots are live, and in every ship group one device has all 8 live. warm_plan is zero on empty slots.
All inputs are finite; a program needn't handle non-finite values.
Results may differ from a plain program's by a relative error of at most 0.0085.
Values sent between devices are 32-bit elements; how exact they have to be, the bound alone decides.
A program may use at most 32 MiB of HBM per device.

v0:
```python
import math

import jax
import jax.numpy as jnp
from jax import lax
from jax.sharding import PartitionSpec as P

ITERS = 3


PRIMAL_DUAL_STEP = 0.5
EPSILON = 1e-06
HIGHEST_PRECISION = lax.Precision.HIGHEST


def on_device(
    tile_cost,
    warm_plan,
    slot_ship,
    slot_truck,
    ship_load,
    truck_limit,
    warm_ship_price,
    warm_truck_price,
):
    slot_count = tile_cost.shape[0]
    tile_size = tile_cost.shape[2]
    ship_blocks = ship_load.shape[1] // tile_size
    truck_blocks = truck_limit.shape[1] // tile_size
    ship_devices = lax.axis_size("ship")
    truck_devices = lax.axis_size("truck")
    row_scale = 1.0 / math.sqrt(tile_size)
    cap_scale = 1.0 / math.sqrt(tile_size * ship_devices)
    cost_tiles = tile_cost.reshape(slot_count, tile_size, tile_size)
    shipment_indicator = (slot_ship == jnp.arange(ship_blocks, dtype=jnp.int32)[None, :]).astype(
        jnp.float32
    )
    truck_onehot = (slot_truck == jnp.arange(truck_blocks, dtype=jnp.int32)[None, :]).astype(
        jnp.float32
    )
    active_flags = jnp.sum(shipment_indicator, axis=1)
    load_blocks = ship_load.reshape(2, ship_blocks, tile_size)
    slot_loads = jnp.einsum(
        "ks,csa->cka", shipment_indicator, load_blocks, precision=HIGHEST_PRECISION
    )
    current_plan = warm_plan.reshape(slot_count, tile_size, tile_size).astype(jnp.float32)
    price_ship = warm_ship_price
    price_truck = warm_truck_price
    weight = jnp.float32(1.0)
    for iteration in range(ITERS):
        primal_update = PRIMAL_DUAL_STEP / weight
        dual_step = PRIMAL_DUAL_STEP * weight
        slot_price = jnp.dot(
            shipment_indicator,
            price_ship.reshape(ship_blocks, tile_size),
            precision=HIGHEST_PRECISION,
        )
        slot_cap = jnp.einsum(
            "kj,cjb->ckb",
            truck_onehot,
            price_truck.reshape(2, truck_blocks, tile_size),
            precision=HIGHEST_PRECISION,
        )
        plan_gradient = (
            cost_tiles.astype(jnp.float32)
            + row_scale * slot_price[:, :, None]
            + cap_scale
            * (
                slot_loads[0][:, :, None] * slot_cap[0][:, None, :]
                + slot_loads[1][:, :, None] * slot_cap[1][:, None, :]
            )
        )
        next_plan = (
            jnp.clip(current_plan - primal_update * plan_gradient, 0.0, 1.0)
            * active_flags[:, None, None]
        )
        reflected = 2.0 * next_plan - current_plan
        slot_rowsum = jnp.sum(reflected, axis=2)
        cap_slot = jnp.einsum("cka,kab->ckb", slot_loads, reflected, precision=HIGHEST_PRECISION)
        cap_part = jnp.einsum(
            "kj,ckb->cjb", truck_onehot, cap_slot, precision=HIGHEST_PRECISION
        ).reshape(2, truck_blocks * tile_size)
        plan_moved = jnp.sum((next_plan - current_plan) ** 2)
        row_part = jnp.dot(shipment_indicator.T, slot_rowsum, precision=HIGHEST_PRECISION).reshape(
            -1
        )
        row_totals = lax.psum(row_part, "truck")
        new_ship = jnp.maximum(price_ship + dual_step * (row_scale * row_totals - row_scale), 0.0)
        cap_totals = lax.psum(cap_part, "ship")
        new_truck = jnp.maximum(
            price_truck + dual_step * (cap_scale * cap_totals - cap_scale * truck_limit), 0.0
        )
        ship_moved = jnp.sum((new_ship - price_ship) ** 2)
        truck_moved = jnp.sum((new_truck - price_truck) ** 2)
        moved_plan, moved_price = lax.psum(
            (plan_moved, ship_moved / truck_devices + truck_moved / ship_devices), ("ship", "truck")
        )
        weight = jnp.sqrt(weight * jnp.sqrt(moved_price + EPSILON) / jnp.sqrt(moved_plan + EPSILON))
        current_plan, price_ship, price_truck = (next_plan, new_ship, new_truck)
    return (
        current_plan.reshape(slot_count, 1, tile_size, tile_size),
        price_ship,
        price_truck,
        weight,
    )


def solution(mesh):
    in_specs = (
        P("ship", "truck", None, None),
        P("ship", "truck", None, None),
        P("ship", "truck"),
        P("ship", "truck"),
        P(None, "ship"),
        P(None, "truck"),
        P("ship"),
        P(None, "truck"),
    )
    out_specs = (P("ship", "truck", None, None), P("ship"), P(None, "truck"), P())
    return jax.shard_map(
        on_device, mesh=mesh, in_specs=in_specs, out_specs=out_specs, check_vma=False
    )
```

profile of v0, /device:TPU:1, one launch (start us, length us, event | category | flops | bytes accessed | tf_op | source)
XLA Modules:
  0.0 1236.5 jit_solution(13819009989218933075)
XLA Ops:
  0.6 1.0 convolution_bitcast_fusion.9
  1.6 0.7 reshape.107
  2.4 0.9 convolution_bitcast_fusion.8
  3.2 0.7 reshape.105
  4.0 0.8 convolution_multiply_fusion.2
  4.8 0.8 convert_reduce_fusion
  5.7 3.9 fusion.36
  9.8 251.0 %psum.85 = f32[2,1536]{1,0:T(2,128)S(1)} all-reduce(f32[2,1536]{1,0:T(2,128)S(1)} %bitcast.271), channel_id=1, replica_groups=mesh['ship'=64,'truck'=12] {'ship'}, use_global_device_ids=true, to_apply=%region_4.5 | all-reduce | flops 3072 | bytes 24576 | tf_op jit(solution)/shard_map/psum | solution.py:89
  262.1 2.3 fusion.9
  264.7 37.9 %psum.84 = f32[6144]{0:T(1024)S(1)} all-reduce(f32[6144]{0:T(1024)S(1)} %bitcast.268), channel_id=1, replica_groups=mesh['ship'=64,'truck'=12] {'truck'}, use_global_device_ids=true, to_apply=%region_2.3 | all-reduce | flops 6144 | bytes 49152 | tf_op jit(solution)/shard_map/psum | solution.py:87
  303.8 119.3 %all-reduce.2 = (f32[]{:T(128)}, f32[]{:T(128)}) all-reduce(f32[]{:T(128)S(6)} %add.175, f32[]{:T(128)} %get-tuple-element.6), channel_id=1, replica_groups=mesh['ship'=64,'truck'=12] {'ship','truck'}, use_global_device_ids=true, to_apply=%region_6.7 | all-reduce | flops 2 | bytes 16 | tf_op jit(solution)/shard_map/psum | solution.py:95
  425.0 3.3 multiply_reduce_fusion.1
  428.6 31.3 %psum.88 = f32[6144]{0:T(1024)S(1)} all-reduce(f32[6144]{0:T(1024)S(1)} %bitcast.269), channel_id=1, replica_groups=mesh['ship'=64,'truck'=12] {'truck'}, use_global_device_ids=true, to_apply=%region_10.11 | all-reduce | flops 6144 | bytes 49152 | tf_op jit(solution)/shard_map/psum | solution.py:87
  461.1 3.6 fusion.41
  464.8 251.7 %psum.89 = f32[2,1536]{1,0:T(2,128)S(1)} all-reduce(f32[2,1536]{1,0:T(2,128)S(1)} %bitcast.272), channel_id=1, replica_groups=mesh['ship'=64,'truck'=12] {'ship'}, use_global_device_ids=true, to_apply=%region_12.13 | all-reduce | flops 3072 | bytes 24576 | tf_op jit(solution)/shard_map/psum | solution.py:89
  717.8 108.7 %all-reduce.1 = (f32[]{:T(128)}, f32[]{:T(128)}) all-reduce(f32[]{:T(128)S(6)} %add.188, f32[]{:T(128)} %get-tuple-element.4), channel_id=1, replica_groups=mesh['ship'=64,'truck'=12] {'ship','truck'}, use_global_device_ids=true, to_apply=%region_14.15 | all-reduce | flops 2 | bytes 16 | tf_op jit(solution)/shard_map/psum | solution.py:95
  828.4 4.1 fusion.82
  832.5 1.2 fusion.51
  833.8 242.1 %psum.93 = f32[2,1536]{1,0:T(2,128)S(1)} all-reduce(f32[2,1536]{1,0:T(2,128)S(1)} %bitcast.273), channel_id=1, replica_groups=mesh['ship'=64,'truck'=12] {'ship'}, use_global_device_ids=true, to_apply=%region_19.20 | all-reduce | flops 3072 | bytes 24576 | tf_op jit(solution)/shard_map/psum | solution.py:89
  1075.9 1.2 multiply_reduce_fusion.5
  1078.0 31.0 %psum.92 = f32[6144]{0:T(1024)S(1)} all-reduce(f32[6144]{0:T(1024)S(1)} %bitcast.270), channel_id=1, replica_groups=mesh['ship'=64,'truck'=12] {'truck'}, use_global_device_ids=true, to_apply=%region_18.19 | all-reduce | flops 6144 | bytes 49152 | tf_op jit(solution)/shard_map/psum | solution.py:87
  1109.1 1.2 multiply_reduce_fusion.2
  1110.9 119.4 %all-reduce = (f32[]{:T(128)}, f32[]{:T(128)}) all-reduce(f32[]{:T(128)S(6)} %add.201, f32[]{:T(128)} %get-tuple-element.28), channel_id=1, replica_groups=mesh['ship'=64,'truck'=12] {'ship','truck'}, use_global_device_ids=true, to_apply=%region_22.23 | all-reduce | flops 2 | bytes 16 | tf_op jit(solution)/shard_map/psum | solution.py:95
  1231.8 3.6 fusion.14
  (41 shorter events, 4.6 us)
Async XLA Ops:
  5.7 3.9 copy-start.5
  5.7 255.1 %copy-start.2 = (f32[2,1536]{1,0:T(2,128)S(1)}, f32[2,1536]{1,0:T(2,128)}, u32[]{:S(2)}) copy-start(f32[2,1536]{1,0:T(2,128)} %param.13) | copy-start | bytes 36868
  5.7 255.1 %copy-start.4 = (f32[2,1536]{1,0:T(2,128)S(1)}, f32[2,1536]{1,0:T(2,128)}, u32[]{:S(2)}) copy-start(f32[2,1536]{1,0:T(2,128)} %param.15) | copy-start | bytes 36868
  5.7 256.4 %copy-start = (bf16[8,1,256,256]{3,2,1,0:T(8,128)(2,1)S(1)}, bf16[8,1,256,256]{3,2,1,0:T(8,128)(2,1)}, u32[]{:S(2)}) copy-start(bf16[8,1,256,256]{3,2,1,0:T(8,128)(2,1)} %param.9) | copy-start | bytes 3145732
  5.7 256.4 %copy-start.1 = (bf16[8,1,256,256]{3,2,1,0:T(8,128)(2,1)S(1)}, bf16[8,1,256,256]{3,2,1,0:T(8,128)(2,1)}, u32[]{:S(2)}) copy-start(bf16[8,1,256,256]{3,2,1,0:T(8,128)(2,1)} %param.8) | copy-start | bytes 3145732
  9.6 254.8 %copy-start.6 = (s32[8,1]{0,1:T(1,128)S(1)}, s32[8,1]{0,1:T(1,128)}, u32[]{:S(2)}) copy-start(s32[8,1]{0,1:T(1,128)} %param.10) | copy-start | bytes 100
  9.6 292.9 %copy-start.3 = (f32[6144]{0:T(1024)S(1)}, f32[6144]{0:T(1024)}, u32[]{:S(2)}) copy-start(f32[6144]{0:T(1024)} %param.14) | copy-start | bytes 73732
where the time goes:
time: 1240 us
  blocking collectives  1190 us (96%)
  other arithmetic  19 us (2%)
  matrix products  13.3 us (1%)
    psum x3, blocking collectives, on_device(): cap_totals = lax.psum(cap_part, 'ship')  745 us
    psum x3, blocking collectives, on_device(): lax.psum((plan_moved, ship_moved / truck_devices + truck_moved / ship_dev...  347 us
    psum x3, blocking collectives, on_device(): row_totals = lax.psum(row_part, 'truck')  100 us

commit v1 on v0

v1 whole, which is shorter than its diff:
```python
import functools
import math

import jax
import jax.numpy as jnp
from jax import lax
from jax.experimental import pallas as pl
from jax.experimental.pallas import tpu as pltpu
from jax.sharding import PartitionSpec as P

MESH = pl.DeviceIdType.MESH
ITERS = 3
STEP = 0.5
EPS = 1e-06
NX, NY, NC, NZ = 4, 8, 2, 12
SHIP = NX * NY * NC
OWNERS = NX * NC
SLOTS, TILE, SB, TB = 8, 256, 24, 6
HALF = TILE // 2
ROWS = 32
F32, BF16 = jnp.float32, jnp.bfloat16


def split(v):
    hi = v.astype(BF16).astype(F32)
    return hi, v - hi


def tree(parts):
    while len(parts) > 1:
        parts = [a + b for a, b in zip(parts[::2], parts[1::2])] + (
            [parts[-1]] if len(parts) % 2 else []
        )
    return parts[0]


def kernel(
    cost_hbm,
    warm_hbm,
    ss_ref,
    st_ref,
    load_ref,
    lim_ref,
    u_ref,
    p_ref,
    x_out,
    u_out,
    p_out,
    w_out,
    cost,
    warm,
    xs,
    gs,
    zh,
    zl,
    hh,
    hl,
    lb,
    at,
    oh,
    us,
    limtab,
    ptab,
    loadk,
    wv,
    sb_l,
    rb_l,
    sb_r,
    rb_r,
    sb_x,
    rb_x,
    sb_o,
    rb_o,
    sb_s,
    rb_s,
    sb_q,
    rb_q,
    in_sem,
    out_sem,
    send_sem,
    l_sem,
    r_sem,
    x_sem,
    o_sem,
    s_sem,
    q_sem,
    p_sem,
):
    i, j = lax.axis_index("ship"), lax.axis_index("truck")
    c = lax.rem(i, NC)
    y = lax.rem(lax.div(i, NC), NY)
    x = lax.div(i, NC * NY)
    own = x * NC + c
    row_scale = 1.0 / math.sqrt(TILE)
    cap_scale = 1.0 / math.sqrt(TILE * SHIP)

    loads_in = []
    for k in range(SLOTS):
        a = pltpu.make_async_copy(cost_hbm.at[k], cost.at[k], in_sem.at[0, k])
        b = pltpu.make_async_copy(warm_hbm.at[k], warm.at[k], in_sem.at[1, k])
        a.start()
        b.start()
        loads_in += [a, b]

    def place(ox, oy, oc):
        px, pc = lax.rem(x + ox, NX), lax.rem(c + oc, NC)
        return (px * NY + lax.rem(y + oy, NY)) * NC + pc, px * NC + pc

    cells = [(ox, oc) for ox in (2, 1, 3, 0) for oc in (1, 0)]

    def each_ship(act):
        def line(n, carry):
            half = (n + 1) // 2
            oy = jnp.where(n % 2 == 1, NY // 2 - half, NY // 2 + half)
            for ox, oc in cells:
                act(*place(ox, oy, oc))
            return carry

        lax.fori_loop(0, NY - 1, line, 0)
        for ox, oc in cells[:-1]:
            act(*place(ox, 0, oc))

    def z_at(n):
        half = (n + 1) // 2
        return lax.rem(j + jnp.where(n % 2 == 1, NZ // 2 - half, NZ // 2 + half), NZ)

    def each_truck(act):
        def line(n, carry):
            act(z_at(n))
            return carry

        lax.fori_loop(0, NZ - 1, line, 0)

    def each_owner(act):
        def line(n, carry):
            for ox, oc in cells:
                act(place(ox, 0, oc)[0], z_at(n))
            return carry

        lax.fori_loop(0, NZ - 1, line, 0)
        for ox, oc in cells[:-1]:
            act(place(ox, 0, oc)[0], j)

    barrier = pltpu.get_barrier_semaphore()

    def greet(di, dj):
        pl.semaphore_signal(barrier, inc=1, device_id=(di, dj), device_id_type=MESH)

    each_ship(lambda di, d: greet(di, j))

    def greet_line(n, carry):
        for ox, oc in cells:
            greet(place(ox, 0, oc)[0], z_at(n))
        return carry

    lax.fori_loop(0, NZ - 1, greet_line, 0)

    def send(src, dst, sem, kind, it, di, dj):
        pltpu.make_async_remote_copy(
            src_ref=src,
            dst_ref=dst,
            send_sem=send_sem.at[kind, it],
            recv_sem=sem,
            device_id=(di, dj),
            device_id_type=MESH,
        ).start()

    def wait(buf, sem):
        pltpu.make_async_copy(buf, buf, sem).wait()

    ship_of = jnp.broadcast_to(ss_ref[...], (SLOTS, TILE))
    truck_of = jnp.broadcast_to(st_ref[...], (SLOTS, TILE))
    sub = lax.broadcasted_iota(jnp.int32, (SLOTS, TILE), 0)
    for h in range(2):
        us[:, h * HALF : (h + 1) * HALF] = u_ref[pl.ds(h, SB, stride=2), :]
    for d in range(OWNERS):
        g, h = d // 2, d % 2
        for r in range(3):
            col = ((g % 2) * 3 + r) * TILE + h * HALF
            limtab[d, r : r + 1, :] = lim_ref[g // 2 : g // 2 + 1, col : col + HALF]
            ptab[0, d, r : r + 1, :] = p_ref[g // 2 : g // 2 + 1, col : col + HALF]
    for n in range(2):
        acc = jnp.zeros((SLOTS, TILE), F32)
        for s in range(SB):
            acc = jnp.where(
                ship_of == s, load_ref[n : n + 1, s * TILE : (s + 1) * TILE], acc
            )
        loadk[n] = acc
    for k in range(SLOTS):
        truck_k = jnp.broadcast_to(st_ref[k : k + 1, :], (SLOTS, TILE))
        hi, lo = [], []
        for g in range(4):
            v = jnp.broadcast_to(loadk[g // 2, k : k + 1, :], (SLOTS, TILE))
            v = jnp.where((sub < 3) & (truck_k == sub + 3 * (g % 2)), v, 0.0)
            a, b = split(v)
            hi.append(a)
            lo.append(b)
        lb[k] = jnp.concatenate(hi + lo, axis=0).astype(BF16)
    sb_o[...] = jnp.broadcast_to(ss_ref[...], (SLOTS, HALF)).astype(F32)
    rb_o[j] = sb_o[...]
    one_row = lax.broadcasted_iota(jnp.int32, (16, HALF), 0)

    def prices_u():
        u8 = jnp.zeros((SLOTS, TILE), F32)
        for s in range(SB):
            u8 = jnp.where(ship_of == s, us[s : s + 1, :], u8)
        u_hi, u_lo = split(u8)
        a_hi, a_lo = split(loadk[0])
        b_hi, b_lo = split(loadk[1])
        stack = [u_hi, u_lo, a_hi, a_lo, a_hi, b_hi, b_lo, b_hi]
        stack.append(jnp.zeros((128 - 8 * len(stack), TILE), F32))
        at[...] = jnp.transpose(jnp.concatenate(stack, axis=0)).astype(BF16)

    def gradient(it):
        parts = []
        for n in range(2):
            p8 = []
            for h in range(2):
                acc = jnp.zeros((SLOTS, HALF), F32)
                for t in range(TB):
                    d = (2 * n + t // 3) * 2 + h
                    acc = jnp.where(
                        truck_of[:, :HALF] == t, ptab[it, d, t % 3 : t % 3 + 1, :], acc
                    )
                p8.append(acc)
            p_hi, p_lo = split(jnp.concatenate(p8, axis=1) * cap_scale)
            parts += [p_hi, p_hi, p_lo]
        ones = jnp.full((SLOTS, TILE), row_scale, F32)
        parts = [ones, ones] + parts
        for k in range(SLOTS):
            rows = [jnp.where(sub == k, v, 0.0) for v in parts]
            rows.append(jnp.zeros((128 - 8 * len(rows), TILE), F32))
            b_k = jnp.concatenate(rows, axis=0).astype(BF16)
            live = jnp.broadcast_to(ss_ref[k : k + 1, :], (HALF, TILE)) >= 0
            for a in range(0, TILE, HALF):
                v = jnp.dot(at[a : a + HALF, :], b_k, preferred_element_type=F32)
                v = v + cost[k, a : a + HALF, :].astype(F32)
                gs[k, a : a + HALF, :] = jnp.where(live, v, 0.0)

    wv[...] = jnp.ones_like(wv)
    prices_u()
    for copy in loads_in:
        copy.wait()
    for k in range(SLOTS):
        xs[k] = warm[k].astype(F32)
    gradient(0)

    pl.semaphore_wait(barrier, SHIP - 1 + (NZ - 1) * OWNERS)
    each_truck(lambda dj: send(sb_o, rb_o.at[j], o_sem.at[0], 4, 0, i, dj))

    def iteration(it, carry):
        weight = wv[...]
        tau = STEP / weight
        sigma = STEP * weight
        moved = jnp.zeros((8, HALF), F32)
        cap_hi = jnp.zeros((64, TILE), F32)
        cap_lo = jnp.zeros((32, TILE), F32)
        rows_acc = jnp.zeros((16, TILE), F32)
        tau_b = jnp.broadcast_to(tau[0:1, 0:1], (ROWS, TILE))
        for k in range(SLOTS):
            for a in range(0, TILE, ROWS):
                old = xs[k, a : a + ROWS, :]
                new = jnp.clip(old - tau_b * gs[k, a : a + ROWS, :], 0.0, 1.0)
                xs[k, a : a + ROWS, :] = new
                step = new - old
                z = new + step
                z_hi = z.astype(BF16)
                zh[k, a : a + ROWS, :] = z_hi
                zl[k, a : a + ROWS, :] = (z - z_hi.astype(F32)).astype(BF16)
                zs = z[:, :HALF] + z[:, HALF:]
                s_hi = zs.astype(BF16)
                hh[k, a : a + ROWS, :] = s_hi
                hl[k, a : a + ROWS, :] = (zs - s_hi.astype(F32)).astype(BF16)
                sq = step * step
                sq = sq[:, :HALF] + sq[:, HALF:]
                moved = moved + jnp.sum(sq.reshape(ROWS // 8, 8, HALF), axis=0)
            cap_hi = cap_hi + jnp.dot(lb[k], zh[k], preferred_element_type=F32)
            cap_lo = cap_lo + jnp.dot(lb[k, :32, :], zl[k], preferred_element_type=F32)
        cap = cap_hi[:32] + cap_hi[32:] + cap_lo
        for d in range(OWNERS):
            g, h = d // 2, d % 2
            sb_l[it, d] = cap[8 * g : 8 * g + 3, h * HALF : (h + 1) * HALF]
        rb_l[it, i] = sb_l[it, own]
        each_ship(
            lambda di, d: send(
                sb_l.at[it, d], rb_l.at[it, i], l_sem.at[it], 0, it, di, j
            )
        )

        nt = (((1,), (1,)), ((), ()))
        for k in range(SLOTS):
            pick = jnp.where(one_row == k, 1.0, 0.0).astype(BF16)
            rows_acc = rows_acc + lax.dot_general(
                pick, hh[k], nt, preferred_element_type=F32
            )
            rows_acc = rows_acc + lax.dot_general(
                pick, hl[k], nt, preferred_element_type=F32
            )
        sb_r[it] = rows_acc[:SLOTS]
        rb_r[it, j] = rows_acc[:SLOTS]
        each_truck(
            lambda dj: send(
                sb_r.at[it], rb_r.at[it, j], r_sem.at[it], 1, it, i, dj
            )
        )
        moved = jnp.sum(moved, axis=0, keepdims=True)
        sb_x[it] = moved
        rb_x[it, j] = moved
        each_truck(
            lambda dj: send(
                sb_x.at[it], rb_x.at[it, j], x_sem.at[it], 2, it, i, dj
            )
        )

        @pl.when(it == ITERS - 1)
        def _():
            pltpu.make_async_copy(xs, x_out, out_sem.at[0]).start()

        wait(rb_l.at[it, pl.ds(0, SHIP - 1)], l_sem.at[it])
        total = tree([rb_l[it, s] for s in range(SHIP)])
        old_p = ptab[it, own]
        sig3 = jnp.broadcast_to(sigma[0:1, 0:1], (3, HALF))
        new_p = jnp.maximum(
            old_p + sig3 * (cap_scale * total - cap_scale * limtab[own]), 0.0
        )
        ptab[it + 1, own] = new_p
        step_p = jnp.sum((new_p - old_p) ** 2, axis=0, keepdims=True)
        sb_s[it] = step_p
        rb_s[it, own * NZ + j] = step_p
        each_owner(
            lambda di, dj: send(
                sb_s.at[it], rb_s.at[it, own * NZ + j], s_sem.at[it], 3, it, di, dj
            )
        )
        for ox, oc in cells[:-1]:
            send(
                ptab.at[it + 1, own],
                ptab.at[it + 1, own],
                p_sem.at[it],
                5,
                it,
                place(ox, 0, oc)[0],
                j,
            )

        @pl.when(it == 0)
        def _():
            wait(rb_o.at[pl.ds(0, NZ - 1)], o_sem.at[0])
            lane = lax.broadcasted_iota(jnp.int32, (NZ * SLOTS, HALF), 1).astype(F32)
            hot = jnp.where(rb_o[...].reshape(NZ * SLOTS, HALF) == lane, 1.0, 0.0)
            hot = jnp.concatenate(
                [hot, jnp.zeros((128 - NZ * SLOTS, HALF), F32)], axis=0
            )
            oh[...] = jnp.transpose(hot)[:32].astype(BF16)

        wait(rb_r.at[it, pl.ds(0, NZ - 1)], r_sem.at[it])
        wait(rb_x.at[it, pl.ds(0, NZ - 1)], x_sem.at[it])
        parts = rb_r[it].reshape(NZ * SLOTS, TILE)
        parts = jnp.concatenate(
            [parts, jnp.zeros((128 - NZ * SLOTS, TILE), F32)], axis=0
        )
        p_hi, p_lo = split(parts)
        rows = jnp.dot(oh[...], p_hi.astype(BF16), preferred_element_type=F32)
        rows = rows + jnp.dot(oh[...], p_lo.astype(BF16), preferred_element_type=F32)
        rows = rows[:SB]
        old_u = us[...]
        sig24 = jnp.broadcast_to(sigma[0:1, 0:1], (SB, TILE))
        new_u = jnp.maximum(old_u + sig24 * (row_scale * rows - row_scale), 0.0)
        us[...] = new_u
        step_u = (new_u - old_u) ** 2
        step_u = jnp.sum(step_u[:, :HALF] + step_u[:, HALF:], axis=0, keepdims=True)
        step_x = tree([rb_x[it, n] for n in range(NZ)])
        step_u = step_u + pltpu.roll(step_u, HALF // 2, 1)
        step_x = step_x + pltpu.roll(step_x, HALF // 2, 1)
        low = lax.broadcasted_iota(jnp.int32, (1, HALF), 1) < HALF // 2
        both = jnp.where(low, step_x, step_u)
        sb_q[it] = both
        rb_q[it, i] = both
        each_ship(
            lambda di, d: send(
                sb_q.at[it], rb_q.at[it, i], q_sem.at[it], 6, it, di, j
            )
        )

        prices_u()
        wait(ptab.at[it + 1, pl.ds(0, OWNERS - 1)], p_sem.at[it])
        gradient(it + 1)
        wait(rb_q.at[it, pl.ds(0, SHIP - 1)], q_sem.at[it])
        q_sum = tree([rb_q[it, s] for s in range(SHIP)])
        wait(rb_s.at[it, pl.ds(0, OWNERS * NZ - 1)], s_sem.at[it])
        s_sum = tree([rb_s[it, s] for s in range(OWNERS * NZ)])
        dx = jnp.sum(jnp.where(low, q_sum, 0.0), axis=1, keepdims=True)
        dy = jnp.sum(jnp.where(low, 0.0, q_sum) + s_sum, axis=1, keepdims=True)
        weight = jnp.sqrt(
            weight[0:1, :]
            * jnp.sqrt(jnp.broadcast_to(dy, (1, HALF)) + EPS)
            / jnp.sqrt(jnp.broadcast_to(dx, (1, HALF)) + EPS)
        )
        wv[...] = jnp.broadcast_to(weight, wv.shape)
        return carry

    lax.fori_loop(0, ITERS, iteration, 0)

    for h in range(2):
        u_out[pl.ds(h, SB, stride=2), :] = us[:, h * HALF : (h + 1) * HALF]
    for d in range(OWNERS):
        g, h = d // 2, d % 2
        for r in range(3):
            col = ((g % 2) * 3 + r) * TILE + h * HALF
            p_out[g // 2 : g // 2 + 1, col : col + HALF] = ptab[ITERS, d, r : r + 1, :]
    w_out[...] = wv[0:1, :]
    for it in range(ITERS):
        wait(rb_l.at[it, pl.ds(0, SHIP - 1)], send_sem.at[0, it])
        wait(rb_r.at[it, pl.ds(0, NZ - 1)], send_sem.at[1, it])
        wait(rb_x.at[it, pl.ds(0, NZ - 1)], send_sem.at[2, it])
        wait(rb_s.at[it, pl.ds(0, OWNERS * NZ - 1)], send_sem.at[3, it])
        wait(ptab.at[it + 1, pl.ds(0, OWNERS - 1)], send_sem.at[5, it])
        wait(rb_q.at[it, pl.ds(0, SHIP - 1)], send_sem.at[6, it])
    wait(rb_o.at[pl.ds(0, NZ - 1)], send_sem.at[4, 0])
    pltpu.make_async_copy(xs, x_out, out_sem.at[0]).wait()


def on_device(cost, warm, slot_ship, slot_truck, load, limit, ship_price, truck_price):
    vmem, hbm = (
        pl.BlockSpec(memory_space=pltpu.VMEM),
        pl.BlockSpec(memory_space=pl.ANY),
    )
    dma = pltpu.SemaphoreType.DMA
    plan, prices, caps, weight = pl.pallas_call(
        kernel,
        out_shape=(
            jax.ShapeDtypeStruct((SLOTS, TILE, TILE), F32),
            jax.ShapeDtypeStruct((2 * SB, HALF), F32),
            jax.ShapeDtypeStruct(truck_price.shape, F32),
            jax.ShapeDtypeStruct((1, HALF), F32),
        ),
        in_specs=[hbm, hbm, vmem, vmem, vmem, vmem, vmem, vmem],
        out_specs=(hbm, vmem, vmem, vmem),
        scratch_shapes=[
            pltpu.VMEM((SLOTS, TILE, TILE), BF16),
            pltpu.VMEM((SLOTS, TILE, TILE), BF16),
            pltpu.VMEM((SLOTS, TILE, TILE), F32),
            pltpu.VMEM((SLOTS, TILE, TILE), F32),
            pltpu.VMEM((SLOTS, TILE, TILE), BF16),
            pltpu.VMEM((SLOTS, TILE, TILE), BF16),
            pltpu.VMEM((SLOTS, TILE, HALF), BF16),
            pltpu.VMEM((SLOTS, TILE, HALF), BF16),
            pltpu.VMEM((SLOTS, 64, TILE), BF16),
            pltpu.VMEM((TILE, 128), BF16),
            pltpu.VMEM((32, 128), BF16),
            pltpu.VMEM((SB, TILE), F32),
            pltpu.VMEM((OWNERS, 3, HALF), F32),
            pltpu.VMEM((ITERS + 1, OWNERS, 3, HALF), F32),
            pltpu.VMEM((2, SLOTS, TILE), F32),
            pltpu.VMEM((8, HALF), F32),
            pltpu.VMEM((ITERS, OWNERS, 3, HALF), F32),
            pltpu.VMEM((ITERS, SHIP, 3, HALF), F32),
            pltpu.VMEM((ITERS, SLOTS, TILE), F32),
            pltpu.VMEM((ITERS, NZ, SLOTS, TILE), F32),
            pltpu.VMEM((ITERS, 1, HALF), F32),
            pltpu.VMEM((ITERS, NZ, 1, HALF), F32),
            pltpu.VMEM((SLOTS, HALF), F32),
            pltpu.VMEM((NZ, SLOTS, HALF), F32),
            pltpu.VMEM((ITERS, 1, HALF), F32),
            pltpu.VMEM((ITERS, OWNERS * NZ, 1, HALF), F32),
            pltpu.VMEM((ITERS, 1, HALF), F32),
            pltpu.VMEM((ITERS, SHIP, 1, HALF), F32),
            dma((2, SLOTS)),
            dma((1,)),
            dma((7, ITERS)),
            dma((ITERS,)),
            dma((ITERS,)),
            dma((ITERS,)),
            dma((1,)),
            dma((ITERS,)),
            dma((ITERS,)),
            dma((ITERS,)),
        ],
        compiler_params=pltpu.CompilerParams(
            collective_id=0, has_side_effects=True, vmem_limit_bytes=40 << 20
        ),
    )(
        cost.reshape(SLOTS, TILE, TILE),
        warm.reshape(SLOTS, TILE, TILE),
        slot_ship,
        slot_truck,
        load,
        limit,
        ship_price.reshape(2 * SB, HALF),
        truck_price,
    )
    return (
        plan.reshape(SLOTS, 1, TILE, TILE),
        prices.reshape(-1),
        caps,
        weight[0, 0],
    )


def solution(mesh):
    in_specs = (
        P("ship", "truck", None, None),
        P("ship", "truck", None, None),
        P("ship", "truck"),
        P("ship", "truck"),
        P(None, "ship"),
        P(None, "truck"),
        P("ship"),
        P(None, "truck"),
    )
    out_specs = (P("ship", "truck", None, None), P("ship"), P(None, "truck"), P())
    return jax.shard_map(
        on_device, mesh=mesh, in_specs=in_specs, out_specs=out_specs, check_vma=False
    )
```

time: 1240 us -> 85.2 us (0.07)
  blocking collectives: 1190 us -> 0 us
  Pallas kernels: 0 us -> 73.5 us
  other arithmetic: 19 us -> 0 us
  matrix products: 13.3 us -> 0 us
    psum x9 -> x0, blocking collectives: 1190 us -> none  [the longest x3 745 us: on_device(): cap_totals = lax.psum(cap_part, 'ship')]
    pallas_call x0 -> x1, Pallas kernels: none -> 73.5 us  [on_device(): pl.pallas_call(kernel, out_shape=(jax.ShapeDtypeStruct((SLOTS, TILE, TILE...]
    reduce_sum x10 -> x0, other arithmetic: 15.4 us -> none  [the longest x2 5.58 us: on_device(): plan_moved = jnp.sum((next_plan - current_plan) ** 2)]
    dot_general x16 -> x0, matrix products: 13.3 us -> none  [the longest x3 8.66 us: on_device(): jnp.einsum('cka,kab->ckb', slot_loads, reflected, precision=HIGHEST_PRECI...]
where the time goes in v1:
time: 85.2 us; the launch traced here: 84.7 us
  Pallas kernels  73.5 us (86%)
  local copies, waits for them, and re-layouts  9.39 us (11%)
  between operations  1.81 us (2%)
    pallas_call x1, Pallas kernels, on_device(): pl.pallas_call(kernel, out_shape=(jax.ShapeDtypeStruct((SLOTS, TILE, TILE...  73.5 us
    unnamed x17, local copies, waits for them, and re-layouts  9.39 us

profile of v1, /device:TPU:1, one launch (start us, length us, event | category | flops | bytes accessed | tf_op | source)
XLA Modules:
  0.0 84.7 jit_solution(13400517989226482976)
XLA Ops:
  0.6 0.7 copy.12.ss_ref
  1.4 0.7 copy.13.st_ref
  2.1 0.0 copy-start
  2.1 1.2 %copy-done = bf16[8,1,256,256]{3,2,1,0:T(8,128)(2,1)S(1)} copy-done((bf16[8,1,256,256]{3,2,1,0:T(8,128)(2,1)S(1)}, bf16[8,1,256,256]{3,2,1,0:T(8,128)(2,1)}, u32[]{:S(2)}) %copy-start) | copy-done | bytes 1048600
  3.3 0.0 copy-start.1
  3.3 1.2 %copy-done.1 = bf16[8,1,256,256]{3,2,1,0:T(8,128)(2,1)S(1)} copy-done((bf16[8,1,256,256]{3,2,1,0:T(8,128)(2,1)S(1)}, bf16[8,1,256,256]{3,2,1,0:T(8,128)(2,1)}, u32[]{:S(2)}) %copy-start.1) | copy-done | bytes 1048600
  4.5 0.0 copy-start.2
  4.5 0.8 copy-done.2
  5.3 0.0 copy-start.3
  5.3 0.7 copy-done.3
  6.1 0.0 copy-start.4
  6.1 0.7 copy-done.4
  6.8 0.0 copy-start.5
  6.8 0.7 copy-done.5
  7.5 73.5 %shard_map.111 = (f32[8,256,256]{2,1,0:T(8,128)S(1)}, f32[48,128]{1,0:T(8,128)S(1)}, f32[2,1536]{1,0:T(2,128)S(1)}, f32[1,128]{1,0:T(1,128)S(1)}) custom-call(bf16[8,256,256]{2,1,0:T(8,128)(2,1)S(1)} %bitcast.10, bf16[8,256,256]{2,1,0:T(8,128)(2,1)S(1)} %bitcast.11, s32[8,1]{1,0:T(8,128)S(1)} %copy.12.ss_ref, s32[8,1]{1,0:T(8,128)S(1)} %copy.13.st_ref, ...), custom_call_target="tpu_custom_call" | custom-call | tf_op jit(solution)/shard_map/pallas_call | solution.py:429
  81.0 1.3 %copy.19 = f32[8,1,256,256]{3,2,1,0:T(8,128)} copy(f32[8,1,256,256]{3,2,1,0:T(8,128)S(1)} %bitcast.9) | data formatting | bytes 4194304
  82.3 0.6 copy.20
  82.9 0.6 copy.21
Async XLA Ops:
  2.1 1.2 %copy-start = (bf16[8,1,256,256]{3,2,1,0:T(8,128)(2,1)S(1)}, bf16[8,1,256,256]{3,2,1,0:T(8,128)(2,1)}, u32[]{:S(2)}) copy-start(bf16[8,1,256,256]{3,2,1,0:T(8,128)(2,1)} %param.8) | copy-start | bytes 3145732
  3.3 1.2 %copy-start.1 = (bf16[8,1,256,256]{3,2,1,0:T(8,128)(2,1)S(1)}, bf16[8,1,256,256]{3,2,1,0:T(8,128)(2,1)}, u32[]{:S(2)}) copy-start(bf16[8,1,256,256]{3,2,1,0:T(8,128)(2,1)} %param.9) | copy-start | bytes 3145732
  4.5 0.8 copy-start.2
  5.3 0.7 copy-start.3
  6.1 0.7 copy-start.4
  6.8 0.7 copy-start.5

commit v2 on v1

--- a/solution.py
+++ b/solution.py
@@ -37,12 +37,12 @@
 def kernel(
     cost_hbm,
     warm_hbm,
-    ss_ref,
-    st_ref,
-    load_ref,
-    lim_ref,
-    u_ref,
-    p_ref,
+    ss_hbm,
+    st_hbm,
+    load_hbm,
+    lim_hbm,
+    u_hbm,
+    p_hbm,
     x_out,
     u_out,
     p_out,
@@ -50,6 +50,12 @@
     cost,
     warm,
     xs,
+    ss_row,
+    st_row,
+    load_ref,
+    lim_ref,
+    u_ref,
+    p_ref,
     gs,
     zh,
     zl,
@@ -62,6 +68,7 @@
     limtab,
     ptab,
     loadk,
+    slot_of,
     wv,
     sb_l,
     rb_l,
@@ -90,23 +97,19 @@
     c = lax.rem(i, NC)
     y = lax.rem(lax.div(i, NC), NY)
     x = lax.div(i, NC * NY)
-    own = x * NC + c
+    own = lax.rem(x + 2 * lax.rem(y, 2), NX) * NC + c
     row_scale = 1.0 / math.sqrt(TILE)
     cap_scale = 1.0 / math.sqrt(TILE * SHIP)
 
-    loads_in = []
-    for k in range(SLOTS):
-        a = pltpu.make_async_copy(cost_hbm.at[k], cost.at[k], in_sem.at[0, k])
-        b = pltpu.make_async_copy(warm_hbm.at[k], warm.at[k], in_sem.at[1, k])
-        a.start()
-        b.start()
-        loads_in += [a, b]
-
     def place(ox, oy, oc):
-        px, pc = lax.rem(x + ox, NX), lax.rem(c + oc, NC)
-        return (px * NY + lax.rem(y + oy, NY)) * NC + pc, px * NC + pc
+        px, py, pc = lax.rem(x + ox, NX), lax.rem(y + oy, NY), lax.rem(c + oc, NC)
+        piece = lax.rem(px + 2 * lax.rem(py, 2), NX) * NC + pc
+        return (px * NY + py) * NC + pc, piece
 
     cells = [(ox, oc) for ox in (2, 1, 3, 0) for oc in (1, 0)]
+    takers = [
+        (ox, oy, oc) for ox, oy in ((1, 0), (3, 0), (0, NY - 1), (0, 0)) for oc in (1, 0)
+    ]
 
     def each_ship(act):
         def line(n, carry):
@@ -131,29 +134,45 @@
 
         lax.fori_loop(0, NZ - 1, line, 0)
 
-    def each_owner(act):
+    def each_taker(act):
         def line(n, carry):
-            for ox, oc in cells:
-                act(place(ox, 0, oc)[0], z_at(n))
+            for at_offset in takers:
+                act(place(*at_offset)[0], z_at(n))
             return carry
 
         lax.fori_loop(0, NZ - 1, line, 0)
-        for ox, oc in cells[:-1]:
-            act(place(ox, 0, oc)[0], j)
+        for at_offset in takers[:-1]:
+            act(place(*at_offset)[0], j)
 
     barrier = pltpu.get_barrier_semaphore()
 
     def greet(di, dj):
         pl.semaphore_signal(barrier, inc=1, device_id=(di, dj), device_id_type=MESH)
 
+    each_truck(lambda dj: greet(i, dj))
     each_ship(lambda di, d: greet(di, j))
 
-    def greet_line(n, carry):
-        for ox, oc in cells:
-            greet(place(ox, 0, oc)[0], z_at(n))
-        return carry
-
-    lax.fori_loop(0, NZ - 1, greet_line, 0)
+    loads_in = [
+        pltpu.make_async_copy(src, dst, in_sem.at[2, n])
+        for n, (src, dst) in enumerate(
+            (
+                (ss_hbm, ss_row),
+                (st_hbm, st_row),
+                (load_hbm, load_ref),
+                (lim_hbm, lim_ref),
+                (u_hbm, u_ref),
+                (p_hbm, p_ref),
+            )
+        )
+    ]
+    tiles_in = []
+    for k in range(SLOTS):
+        tiles_in += [
+            pltpu.make_async_copy(warm_hbm.at[k], warm.at[k], in_sem.at[1, k]),
+            pltpu.make_async_copy(cost_hbm.at[k], cost.at[k], in_sem.at[0, k]),
+        ]
+    for copy in loads_in + tiles_in:
+        copy.start()
 
     def send(src, dst, sem, kind, it, di, dj):
         pltpu.make_async_remote_copy(
@@ -168,8 +187,22 @@
     def wait(buf, sem):
         pltpu.make_async_copy(buf, buf, sem).wait()
 
-    ship_of = jnp.broadcast_to(ss_ref[...], (SLOTS, TILE))
-    truck_of = jnp.broadcast_to(st_ref[...], (SLOTS, TILE))
+    for copy in loads_in:
+        copy.wait()
+    square = (SLOTS, SLOTS)
+    diagonal = lax.broadcasted_iota(jnp.int32, square, 0) == lax.broadcasted_iota(
+        jnp.int32, square, 1
+    )
+
+    def column(row):
+        v = jnp.broadcast_to(row[...].astype(F32), square)
+        return jnp.sum(jnp.where(diagonal, v, 0.0), axis=1, keepdims=True)
+
+    ship_f = jnp.broadcast_to(column(ss_row), (SLOTS, TILE))
+    ship_of = ship_f.astype(jnp.int32)
+    truck_of = jnp.broadcast_to(column(st_row), (SLOTS, TILE)).astype(jnp.int32)
+    slot_of[0] = ship_of
+    slot_of[1] = truck_of
     sub = lax.broadcasted_iota(jnp.int32, (SLOTS, TILE), 0)
     for h in range(2):
         us[:, h * HALF : (h + 1) * HALF] = u_ref[pl.ds(h, SB, stride=2), :]
@@ -187,7 +220,7 @@
             )
         loadk[n] = acc
     for k in range(SLOTS):
-        truck_k = jnp.broadcast_to(st_ref[k : k + 1, :], (SLOTS, TILE))
+        truck_k = jnp.broadcast_to(slot_of[1, k : k + 1, :], (SLOTS, TILE))
         hi, lo = [], []
         for g in range(4):
             v = jnp.broadcast_to(loadk[g // 2, k : k + 1, :], (SLOTS, TILE))
@@ -196,7 +229,7 @@
             hi.append(a)
             lo.append(b)
         lb[k] = jnp.concatenate(hi + lo, axis=0).astype(BF16)
-    sb_o[...] = jnp.broadcast_to(ss_ref[...], (SLOTS, HALF)).astype(F32)
+    sb_o[...] = ship_f[:, :HALF]
     rb_o[j] = sb_o[...]
     one_row = lax.broadcasted_iota(jnp.int32, (16, HALF), 0)
 
@@ -231,7 +264,7 @@
             rows = [jnp.where(sub == k, v, 0.0) for v in parts]
             rows.append(jnp.zeros((128 - 8 * len(rows), TILE), F32))
             b_k = jnp.concatenate(rows, axis=0).astype(BF16)
-            live = jnp.broadcast_to(ss_ref[k : k + 1, :], (HALF, TILE)) >= 0
+            live = jnp.broadcast_to(slot_of[0, k : k + 1, :], (HALF, TILE)) >= 0
             for a in range(0, TILE, HALF):
                 v = jnp.dot(at[a : a + HALF, :], b_k, preferred_element_type=F32)
                 v = v + cost[k, a : a + HALF, :].astype(F32)
@@ -239,13 +272,13 @@
 
     wv[...] = jnp.ones_like(wv)
     prices_u()
-    for copy in loads_in:
+    for copy in tiles_in:
         copy.wait()
     for k in range(SLOTS):
         xs[k] = warm[k].astype(F32)
     gradient(0)
 
-    pl.semaphore_wait(barrier, SHIP - 1 + (NZ - 1) * OWNERS)
+    pl.semaphore_wait(barrier, SHIP - 1 + NZ - 1)
     each_truck(lambda dj: send(sb_o, rb_o.at[j], o_sem.at[0], 4, 0, i, dj))
 
     def iteration(it, carry):
@@ -256,6 +289,7 @@
         cap_hi = jnp.zeros((64, TILE), F32)
         cap_lo = jnp.zeros((32, TILE), F32)
         rows_acc = jnp.zeros((16, TILE), F32)
+        nt = (((1,), (1,)), ((), ()))
         tau_b = jnp.broadcast_to(tau[0:1, 0:1], (ROWS, TILE))
         for k in range(SLOTS):
             for a in range(0, TILE, ROWS):
@@ -274,8 +308,20 @@
                 sq = step * step
                 sq = sq[:, :HALF] + sq[:, HALF:]
                 moved = moved + jnp.sum(sq.reshape(ROWS // 8, 8, HALF), axis=0)
+            pick = jnp.where(one_row == k, 1.0, 0.0).astype(BF16)
+            for v in (hh, hl):
+                rows_acc = rows_acc + lax.dot_general(
+                    pick, v[k], nt, preferred_element_type=F32
+                )
             cap_hi = cap_hi + jnp.dot(lb[k], zh[k], preferred_element_type=F32)
             cap_lo = cap_lo + jnp.dot(lb[k, :32, :], zl[k], preferred_element_type=F32)
+        sb_r[it] = rows_acc[:SLOTS]
+        rb_r[it, j] = rows_acc[:SLOTS]
+        each_truck(
+            lambda dj: send(
+                sb_r.at[it], rb_r.at[it, j], r_sem.at[it], 1, it, i, dj
+            )
+        )
         cap = cap_hi[:32] + cap_hi[32:] + cap_lo
         for d in range(OWNERS):
             g, h = d // 2, d % 2
@@ -286,29 +332,12 @@
                 sb_l.at[it, d], rb_l.at[it, i], l_sem.at[it], 0, it, di, j
             )
         )
-
-        nt = (((1,), (1,)), ((), ()))
-        for k in range(SLOTS):
-            pick = jnp.where(one_row == k, 1.0, 0.0).astype(BF16)
-            rows_acc = rows_acc + lax.dot_general(
-                pick, hh[k], nt, preferred_element_type=F32
-            )
-            rows_acc = rows_acc + lax.dot_general(
-                pick, hl[k], nt, preferred_element_type=F32
-            )
-        sb_r[it] = rows_acc[:SLOTS]
-        rb_r[it, j] = rows_acc[:SLOTS]
+        moved = jnp.sum(moved, axis=0, keepdims=True)
+        sb_x[it] = moved
+        rb_x[it, pl.ds(j, 1)] = moved
         each_truck(
             lambda dj: send(
-                sb_r.at[it], rb_r.at[it, j], r_sem.at[it], 1, it, i, dj
-            )
-        )
-        moved = jnp.sum(moved, axis=0, keepdims=True)
-        sb_x[it] = moved
-        rb_x[it, j] = moved
-        each_truck(
-            lambda dj: send(
-                sb_x.at[it], rb_x.at[it, j], x_sem.at[it], 2, it, i, dj
+                sb_x.at[it], rb_x.at[it, pl.ds(j, 1)], x_sem.at[it], 2, it, i, dj
             )
         )
 
@@ -326,20 +355,20 @@
         ptab[it + 1, own] = new_p
         step_p = jnp.sum((new_p - old_p) ** 2, axis=0, keepdims=True)
         sb_s[it] = step_p
-        rb_s[it, own * NZ + j] = step_p
-        each_owner(
+        rb_s[it, pl.ds(own * NZ + j, 1)] = step_p
+        each_taker(
             lambda di, dj: send(
-                sb_s.at[it], rb_s.at[it, own * NZ + j], s_sem.at[it], 3, it, di, dj
-            )
-        )
-        for ox, oc in cells[:-1]:
+                sb_s.at[it], rb_s.at[it, pl.ds(own * NZ + j, 1)], s_sem.at[it], 3, it, di, dj
+            )
+        )
+        for at_offset in takers[:-1]:
             send(
                 ptab.at[it + 1, own],
                 ptab.at[it + 1, own],
                 p_sem.at[it],
                 5,
                 it,
-                place(ox, 0, oc)[0],
+                place(*at_offset)[0],
                 j,
             )
 
@@ -369,16 +398,16 @@
         us[...] = new_u
         step_u = (new_u - old_u) ** 2
         step_u = jnp.sum(step_u[:, :HALF] + step_u[:, HALF:], axis=0, keepdims=True)
-        step_x = tree([rb_x[it, n] for n in range(NZ)])
+        step_x = jnp.sum(rb_x[it], axis=0, keepdims=True)
         step_u = step_u + pltpu.roll(step_u, HALF // 2, 1)
         step_x = step_x + pltpu.roll(step_x, HALF // 2, 1)
         low = lax.broadcasted_iota(jnp.int32, (1, HALF), 1) < HALF // 2
         both = jnp.where(low, step_x, step_u)
         sb_q[it] = both
-        rb_q[it, i] = both
+        rb_q[it, pl.ds(i, 1)] = both
         each_ship(
             lambda di, d: send(
-                sb_q.at[it], rb_q.at[it, i], q_sem.at[it], 6, it, di, j
+                sb_q.at[it], rb_q.at[it, pl.ds(i, 1)], q_sem.at[it], 6, it, di, j
             )
         )
 
@@ -386,9 +415,9 @@
         wait(ptab.at[it + 1, pl.ds(0, OWNERS - 1)], p_sem.at[it])
         gradient(it + 1)
         wait(rb_q.at[it, pl.ds(0, SHIP - 1)], q_sem.at[it])
-        q_sum = tree([rb_q[it, s] for s in range(SHIP)])
+        q_sum = jnp.sum(rb_q[it], axis=0, keepdims=True)
         wait(rb_s.at[it, pl.ds(0, OWNERS * NZ - 1)], s_sem.at[it])
-        s_sum = tree([rb_s[it, s] for s in range(OWNERS * NZ)])
+        s_sum = jnp.sum(rb_s[it], axis=0, keepdims=True)
         dx = jnp.sum(jnp.where(low, q_sum, 0.0), axis=1, keepdims=True)
         dy = jnp.sum(jnp.where(low, 0.0, q_sum) + s_sum, axis=1, keepdims=True)
         weight = jnp.sqrt(
@@ -420,10 +449,29 @@
     pltpu.make_async_copy(xs, x_out, out_sem.at[0]).wait()
 
 
+def copy_out(*refs):
+    ins, outs, held, in_sem, out_sem = refs[:4], refs[4:8], refs[8:12], *refs[12:]
+    pairs = [(ins[0].at[k], held[0].at[k], outs[0].at[k]) for k in range(SLOTS)]
+    pairs += list(zip(ins[1:], held[1:], outs[1:]))
+    first = [
+        pltpu.make_async_copy(a, b, in_sem.at[n]) for n, (a, b, _) in enumerate(pairs)
+    ]
+    second = [
+        pltpu.make_async_copy(b, c, out_sem.at[n]) for n, (_, b, c) in enumerate(pairs)
+    ]
+    for copy in first:
+        copy.start()
+    for a, b in zip(first, second):
+        a.wait()
+        b.start()
+    for copy in second:
+        copy.wait()
+
+
 def on_device(cost, warm, slot_ship, slot_truck, load, limit, ship_price, truck_price):
     vmem, hbm = (
         pl.BlockSpec(memory_space=pltpu.VMEM),
-        pl.BlockSpec(memory_space=pl.ANY),
+        pl.BlockSpec(memory_space=pltpu.HBM),
     )
     dma = pltpu.SemaphoreType.DMA
     plan, prices, caps, weight = pl.pallas_call(
@@ -434,12 +482,18 @@
             jax.ShapeDtypeStruct(truck_price.shape, F32),
             jax.ShapeDtypeStruct((1, HALF), F32),
         ),
-        in_specs=[hbm, hbm, vmem, vmem, vmem, vmem, vmem, vmem],
+        in_specs=[hbm] * 8,
         out_specs=(hbm, vmem, vmem, vmem),
         scratch_shapes=[
             pltpu.VMEM((SLOTS, TILE, TILE), BF16),
             pltpu.VMEM((SLOTS, TILE, TILE), BF16),
             pltpu.VMEM((SLOTS, TILE, TILE), F32),
+            pltpu.VMEM((1, SLOTS), jnp.int32),
+            pltpu.VMEM((1, SLOTS), jnp.int32),
+            pltpu.VMEM(load.shape, F32),
+            pltpu.VMEM(limit.shape, F32),
+            pltpu.VMEM((2 * SB, HALF), F32),
+            pltpu.VMEM(truck_price.shape, F32),
             pltpu.VMEM((SLOTS, TILE, TILE), F32),
             pltpu.VMEM((SLOTS, TILE, TILE), BF16),
             pltpu.VMEM((SLOTS, TILE, TILE), BF16),
@@ -452,20 +506,21 @@
             pltpu.VMEM((OWNERS, 3, HALF), F32),
             pltpu.VMEM((ITERS + 1, OWNERS, 3, HALF), F32),
             pltpu.VMEM((2, SLOTS, TILE), F32),
+            pltpu.VMEM((2, SLOTS, TILE), jnp.int32),
             pltpu.VMEM((8, HALF), F32),
             pltpu.VMEM((ITERS, OWNERS, 3, HALF), F32),
             pltpu.VMEM((ITERS, SHIP, 3, HALF), F32),
             pltpu.VMEM((ITERS, SLOTS, TILE), F32),
             pltpu.VMEM((ITERS, NZ, SLOTS, TILE), F32),
             pltpu.VMEM((ITERS, 1, HALF), F32),
-            pltpu.VMEM((ITERS, NZ, 1, HALF), F32),
+            pltpu.VMEM((ITERS, NZ, HALF), F32),
             pltpu.VMEM((SLOTS, HALF), F32),
             pltpu.VMEM((NZ, SLOTS, HALF), F32),
             pltpu.VMEM((ITERS, 1, HALF), F32),
-            pltpu.VMEM((ITERS, OWNERS * NZ, 1, HALF), F32),
+            pltpu.VMEM((ITERS, OWNERS * NZ, HALF), F32),
             pltpu.VMEM((ITERS, 1, HALF), F32),
-            pltpu.VMEM((ITERS, SHIP, 1, HALF), F32),
-            dma((2, SLOTS)),
+            pltpu.VMEM((ITERS, SHIP, HALF), F32),
+            dma((3, SLOTS)),
             dma((1,)),
             dma((7, ITERS)),
             dma((ITERS,)),
@@ -477,18 +532,27 @@
             dma((ITERS,)),
         ],
         compiler_params=pltpu.CompilerParams(
-            collective_id=0, has_side_effects=True, vmem_limit_bytes=40 << 20
+            collective_id=0, has_side_effects=True, vmem_limit_bytes=60 << 20
         ),
     )(
         cost.reshape(SLOTS, TILE, TILE),
         warm.reshape(SLOTS, TILE, TILE),
-        slot_ship,
-        slot_truck,
+        slot_ship.reshape(1, SLOTS),
+        slot_truck.reshape(1, SLOTS),
         load,
         limit,
         ship_price.reshape(2 * SB, HALF),
         truck_price,
     )
+    results = (plan, prices, caps, weight)
+    plan, prices, caps, weight = pl.pallas_call(
+        copy_out,
+        out_shape=[jax.ShapeDtypeStruct(v.shape, v.dtype) for v in results],
+        in_specs=[hbm] * 4,
+        out_specs=[hbm] * 4,
+        scratch_shapes=[pltpu.VMEM(v.shape, v.dtype) for v in results]
+        + [dma((SLOTS + 3,)), dma((SLOTS + 3,))],
+    )(*results)
     return (
         plan.reshape(SLOTS, 1, TILE, TILE),
         prices.reshape(-1),

time: 85.2 us -> 71 us (0.83)
  local copies, waits for them, and re-layouts: 9.39 us -> 0 us
  Pallas kernels: 73.5 us -> 70.2 us
  between operations: 1.81 us -> 0.64 us
    unnamed x17 -> x0, local copies, waits for them, and re-layouts: 9.39 us -> none
    pallas_call x1, Pallas kernels: 73.5 us -> 67.7 us  [on_device(): pl.pallas_call(kernel, out_shape=(jax.ShapeDtypeStruct((SLOTS, TILE, TILE...]
    pallas_call x0 -> x1, Pallas kernels: none -> 2.45 us  [on_device(): pl.pallas_call(copy_out, out_shape=[jax.ShapeDtypeStruct(v.shape, v.dtype...]
where the time goes in v2:
time: 71 us; the launch traced here: 70.8 us
  Pallas kernels  70.2 us (99%)
    pallas_call x1, Pallas kernels, on_device(): pl.pallas_call(kernel, out_shape=(jax.ShapeDtypeStruct((SLOTS, TILE, TILE...  67.7 us
    pallas_call x1, Pallas kernels, on_device(): pl.pallas_call(copy_out, out_shape=[jax.ShapeDtypeStruct(v.shape, v.dtype...  2.45 us

profile of v2, /device:TPU:1, one launch (start us, length us, event | category | flops | bytes accessed | tf_op | source)
XLA Modules:
  0.0 70.8 jit_solution(5159291886680537444)
XLA Ops:
  0.6 67.7 %shard_map.111 = (f32[8,256,256]{2,1,0:T(8,128)}, f32[48,128]{1,0:T(8,128)}, f32[2,1536]{1,0:T(2,128)}, f32[1,128]{1,0:T(1,128)}) custom-call(bf16[8,256,256]{2,1,0:T(8,128)(2,1)} %bitcast.11, bf16[8,256,256]{2,1,0:T(8,128)(2,1)} %bitcast.12, s32[1,8]{1,0:T(1,128)} %bitcast.14, s32[1,8]{1,0:T(1,128)} %bitcast.15, f32[2,6144]{1,0:T(2,128)} %load_hbm.1, ...), custom_call_target="tpu_custom_call" | custom-call | tf_op jit(solution)/shard_map/pallas_call | solution.py:477
  68.4 2.5 %shard_map.112 = (f32[8,256,256]{2,1,0:T(8,128)}, f32[48,128]{1,0:T(8,128)}, f32[2,1536]{1,0:T(2,128)}, f32[1,128]{1,0:T(1,128)}) custom-call(f32[8,256,256]{2,1,0:T(8,128)} %get-tuple-element.12.refs_0_, f32[48,128]{1,0:T(8,128)} %get-tuple-element.13.refs_1_, f32[2,1536]{1,0:T(2,128)} %get-tuple-element.14.refs_2_, f32[1,128]{1,0:T(1,128)} %get-tuple-element.15.refs_3_), custom_call_target="tpu_custom_call" | custom-call | tf_op jit(solution)/shard_map/pallas_call | solution.py:548

commit v3 on v2

--- a/solution.py
+++ b/solution.py
@@ -17,7 +17,7 @@
 OWNERS = NX * NC
 SLOTS, TILE, SB, TB = 8, 256, 24, 6
 HALF = TILE // 2
-ROWS = 32
+ROWS = 16
 F32, BF16 = jnp.float32, jnp.bfloat16
 
 
@@ -60,7 +60,6 @@
     zh,
     zl,
     hh,
-    hl,
     lb,
     at,
     oh,
@@ -69,6 +68,8 @@
     ptab,
     loadk,
     slot_of,
+    u_fin,
+    p_fin,
     wv,
     sb_l,
     rb_l,
@@ -231,7 +232,7 @@
         lb[k] = jnp.concatenate(hi + lo, axis=0).astype(BF16)
     sb_o[...] = ship_f[:, :HALF]
     rb_o[j] = sb_o[...]
-    one_row = lax.broadcasted_iota(jnp.int32, (16, HALF), 0)
+    one_row = lax.broadcasted_iota(jnp.int32, (16, TILE), 0)
 
     def prices_u():
         u8 = jnp.zeros((SLOTS, TILE), F32)
@@ -303,18 +304,25 @@
                 zl[k, a : a + ROWS, :] = (z - z_hi.astype(F32)).astype(BF16)
                 zs = z[:, :HALF] + z[:, HALF:]
                 s_hi = zs.astype(BF16)
-                hh[k, a : a + ROWS, :] = s_hi
-                hl[k, a : a + ROWS, :] = (zs - s_hi.astype(F32)).astype(BF16)
+                hh[k, a : a + ROWS, :HALF] = s_hi
+                hh[k, a : a + ROWS, HALF:] = (zs - s_hi.astype(F32)).astype(BF16)
                 sq = step * step
                 sq = sq[:, :HALF] + sq[:, HALF:]
                 moved = moved + jnp.sum(sq.reshape(ROWS // 8, 8, HALF), axis=0)
-            pick = jnp.where(one_row == k, 1.0, 0.0).astype(BF16)
-            for v in (hh, hl):
-                rows_acc = rows_acc + lax.dot_general(
-                    pick, v[k], nt, preferred_element_type=F32
-                )
-            cap_hi = cap_hi + jnp.dot(lb[k], zh[k], preferred_element_type=F32)
-            cap_lo = cap_lo + jnp.dot(lb[k, :32, :], zl[k], preferred_element_type=F32)
+            if k == 0:
+                continue
+            pick = jnp.where(one_row == k - 1, 1.0, 0.0).astype(BF16)
+            rows_acc = rows_acc + lax.dot_general(
+                pick, hh[k - 1], nt, preferred_element_type=F32
+            )
+            cap_hi = cap_hi + jnp.dot(lb[k - 1], zh[k - 1], preferred_element_type=F32)
+            cap_lo = cap_lo + jnp.dot(lb[k - 1, :32, :], zl[k - 1], preferred_element_type=F32)
+        pick = jnp.where(one_row == SLOTS - 1, 1.0, 0.0).astype(BF16)
+        rows_acc = rows_acc + lax.dot_general(
+            pick, hh[SLOTS - 1], nt, preferred_element_type=F32
+        )
+        cap_hi = cap_hi + jnp.dot(lb[SLOTS - 1], zh[SLOTS - 1], preferred_element_type=F32)
+        cap_lo = cap_lo + jnp.dot(lb[SLOTS - 1, :32, :], zl[SLOTS - 1], preferred_element_type=F32)
         sb_r[it] = rows_acc[:SLOTS]
         rb_r[it, j] = rows_acc[:SLOTS]
         each_truck(
@@ -380,27 +388,32 @@
             hot = jnp.concatenate(
                 [hot, jnp.zeros((128 - NZ * SLOTS, HALF), F32)], axis=0
             )
-            oh[...] = jnp.transpose(hot)[:32].astype(BF16)
-
+            hot = jnp.transpose(hot)[:32].astype(BF16)
+            oh[...] = jnp.concatenate([hot, hot], axis=1)
+
+        wait(rb_x.at[it, pl.ds(0, NZ - 1)], x_sem.at[it])
+        step_x = jnp.sum(rb_x[it], axis=0, keepdims=True)
+        step_x = step_x + pltpu.roll(step_x, HALF // 2, 1)
         wait(rb_r.at[it, pl.ds(0, NZ - 1)], r_sem.at[it])
-        wait(rb_x.at[it, pl.ds(0, NZ - 1)], x_sem.at[it])
-        parts = rb_r[it].reshape(NZ * SLOTS, TILE)
-        parts = jnp.concatenate(
-            [parts, jnp.zeros((128 - NZ * SLOTS, TILE), F32)], axis=0
-        )
-        p_hi, p_lo = split(parts)
-        rows = jnp.dot(oh[...], p_hi.astype(BF16), preferred_element_type=F32)
-        rows = rows + jnp.dot(oh[...], p_lo.astype(BF16), preferred_element_type=F32)
+        p_hi, p_lo = split(rb_r[it].reshape(NZ * SLOTS, TILE))
+        gap = jnp.zeros((128 - NZ * SLOTS, TILE), F32)
+        parts = jnp.concatenate([p_hi, gap, p_lo, gap], axis=0).astype(BF16)
+        rows = jnp.dot(oh[...], parts, preferred_element_type=F32)
         rows = rows[:SB]
         old_u = us[...]
         sig24 = jnp.broadcast_to(sigma[0:1, 0:1], (SB, TILE))
         new_u = jnp.maximum(old_u + sig24 * (row_scale * rows - row_scale), 0.0)
         us[...] = new_u
+
+        @pl.when(it == ITERS - 1)
+        def _():
+            for h in range(2):
+                u_fin[pl.ds(h, SB, stride=2), :] = new_u[:, h * HALF : (h + 1) * HALF]
+            pltpu.make_async_copy(u_fin, u_out, out_sem.at[1]).start()
+
         step_u = (new_u - old_u) ** 2
         step_u = jnp.sum(step_u[:, :HALF] + step_u[:, HALF:], axis=0, keepdims=True)
-        step_x = jnp.sum(rb_x[it], axis=0, keepdims=True)
         step_u = step_u + pltpu.roll(step_u, HALF // 2, 1)
-        step_x = step_x + pltpu.roll(step_x, HALF // 2, 1)
         low = lax.broadcasted_iota(jnp.int32, (1, HALF), 1) < HALF // 2
         both = jnp.where(low, step_x, step_u)
         sb_q[it] = both
@@ -413,6 +426,18 @@
 
         prices_u()
         wait(ptab.at[it + 1, pl.ds(0, OWNERS - 1)], p_sem.at[it])
+
+        @pl.when(it == ITERS - 1)
+        def _():
+            for d in range(OWNERS):
+                g, h = d // 2, d % 2
+                for r in range(3):
+                    col = ((g % 2) * 3 + r) * TILE + h * HALF
+                    p_fin[g // 2 : g // 2 + 1, col : col + HALF] = ptab[
+                        it + 1, d, r : r + 1, :
+                    ]
+            pltpu.make_async_copy(p_fin, p_out, out_sem.at[2]).start()
+
         gradient(it + 1)
         wait(rb_q.at[it, pl.ds(0, SHIP - 1)], q_sem.at[it])
         q_sum = jnp.sum(rb_q[it], axis=0, keepdims=True)
@@ -430,13 +455,6 @@
 
     lax.fori_loop(0, ITERS, iteration, 0)
 
-    for h in range(2):
-        u_out[pl.ds(h, SB, stride=2), :] = us[:, h * HALF : (h + 1) * HALF]
-    for d in range(OWNERS):
-        g, h = d // 2, d % 2
-        for r in range(3):
-            col = ((g % 2) * 3 + r) * TILE + h * HALF
-            p_out[g // 2 : g // 2 + 1, col : col + HALF] = ptab[ITERS, d, r : r + 1, :]
     w_out[...] = wv[0:1, :]
     for it in range(ITERS):
         wait(rb_l.at[it, pl.ds(0, SHIP - 1)], send_sem.at[0, it])
@@ -447,6 +465,8 @@
         wait(rb_q.at[it, pl.ds(0, SHIP - 1)], send_sem.at[6, it])
     wait(rb_o.at[pl.ds(0, NZ - 1)], send_sem.at[4, 0])
     pltpu.make_async_copy(xs, x_out, out_sem.at[0]).wait()
+    pltpu.make_async_copy(u_fin, u_out, out_sem.at[1]).wait()
+    pltpu.make_async_copy(p_fin, p_out, out_sem.at[2]).wait()
 
 
 def copy_out(*refs):
@@ -483,7 +503,7 @@
             jax.ShapeDtypeStruct((1, HALF), F32),
         ),
         in_specs=[hbm] * 8,
-        out_specs=(hbm, vmem, vmem, vmem),
+        out_specs=(hbm, hbm, hbm, vmem),
         scratch_shapes=[
             pltpu.VMEM((SLOTS, TILE, TILE), BF16),
             pltpu.VMEM((SLOTS, TILE, TILE), BF16),
@@ -497,16 +517,17 @@
             pltpu.VMEM((SLOTS, TILE, TILE), F32),
             pltpu.VMEM((SLOTS, TILE, TILE), BF16),
             pltpu.VMEM((SLOTS, TILE, TILE), BF16),
-            pltpu.VMEM((SLOTS, TILE, HALF), BF16),
-            pltpu.VMEM((SLOTS, TILE, HALF), BF16),
+            pltpu.VMEM((SLOTS, TILE, TILE), BF16),
             pltpu.VMEM((SLOTS, 64, TILE), BF16),
             pltpu.VMEM((TILE, 128), BF16),
-            pltpu.VMEM((32, 128), BF16),
+            pltpu.VMEM((32, 256), BF16),
             pltpu.VMEM((SB, TILE), F32),
             pltpu.VMEM((OWNERS, 3, HALF), F32),
             pltpu.VMEM((ITERS + 1, OWNERS, 3, HALF), F32),
             pltpu.VMEM((2, SLOTS, TILE), F32),
             pltpu.VMEM((2, SLOTS, TILE), jnp.int32),
+            pltpu.VMEM((2 * SB, HALF), F32),
+            pltpu.VMEM(truck_price.shape, F32),
             pltpu.VMEM((8, HALF), F32),
             pltpu.VMEM((ITERS, OWNERS, 3, HALF), F32),
             pltpu.VMEM((ITERS, SHIP, 3, HALF), F32),
@@ -521,7 +542,7 @@
             pltpu.VMEM((ITERS, 1, HALF), F32),
             pltpu.VMEM((ITERS, SHIP, HALF), F32),
             dma((3, SLOTS)),
-            dma((1,)),
+            dma((3,)),
             dma((7, ITERS)),
             dma((ITERS,)),
             dma((ITERS,)),

time: 71 us -> 71.4 us (level)
  no operation moved by 1% of the time
where the time goes in v3:
time: 71.4 us; the launch traced here: 71.2 us
  Pallas kernels  70.5 us (99%)
    pallas_call x1, Pallas kernels, on_device(): pl.pallas_call(kernel, out_shape=(jax.ShapeDtypeStruct((SLOTS, TILE, TILE...  68.1 us
    pallas_call x1, Pallas kernels, on_device(): pl.pallas_call(copy_out, out_shape=[jax.ShapeDtypeStruct(v.shape, v.dtype...  2.45 us

profile of v3, /device:TPU:1, one launch (start us, length us, event | category | flops | bytes accessed | tf_op | source)
XLA Modules:
  0.0 71.2 jit_solution(111911996264081735)
XLA Ops:
  0.6 68.1 %shard_map.111 = (f32[8,256,256]{2,1,0:T(8,128)}, f32[48,128]{1,0:T(8,128)}, f32[2,1536]{1,0:T(2,128)}, f32[1,128]{1,0:T(1,128)}) custom-call(bf16[8,256,256]{2,1,0:T(8,128)(2,1)} %bitcast.11, bf16[8,256,256]{2,1,0:T(8,128)(2,1)} %bitcast.12, s32[1,8]{1,0:T(1,128)} %bitcast.14, s32[1,8]{1,0:T(1,128)} %bitcast.15, f32[2,6144]{1,0:T(2,128)} %load_hbm.1, ...), custom_call_target="tpu_custom_call" | custom-call | tf_op jit(solution)/shard_map/pallas_call | solution.py:497
  68.7 2.5 %shard_map.112 = (f32[8,256,256]{2,1,0:T(8,128)}, f32[48,128]{1,0:T(8,128)}, f32[2,1536]{1,0:T(2,128)}, f32[1,128]{1,0:T(1,128)}) custom-call(f32[8,256,256]{2,1,0:T(8,128)} %get-tuple-element.12.refs_0_, f32[48,128]{1,0:T(8,128)} %get-tuple-element.13.refs_1_, f32[2,1536]{1,0:T(2,128)} %get-tuple-element.14.refs_2_, f32[1,128]{1,0:T(1,128)} %get-tuple-element.15.refs_3_), custom_call_target="tpu_custom_call" | custom-call | tf_op jit(solution)/shard_map/pallas_call | solution.py:569
